TPU v7x, 32 devices: a whole 2x2x4 slice. The times are simulated.
32 devices in a mesh: fsdp: 8 (over y, x, core), group: 4 (over z).
Axes of the slice: x: 2, y: 2, z: 4, core: 2. Of those that a mesh axis runs over, the one named last changes fastest.
Arguments:
- gradients: bfloat16 [32, 512, 512], P('group', 'fsdp'), may hold values from -6 to 6
- owners: int32 [4, 8], P('group'), may hold values from 0 to 7, each once within a row
- left_factors: float32 [32, 512, 512], P(('fsdp', 'group')), may hold values from -60 to 800, as said below
- right_factors: float32 [32, 512, 512], P(('fsdp', 'group')), may hold values from -60 to 800, as said below
- left_bases: float32 [32, 512, 512], P(('fsdp', 'group')), may hold values from -1 to 1
- right_bases: float32 [32, 512, 512], P(('fsdp', 'group')), may hold values from -1 to 1
- moments: float32 [32, 512, 512], P(('fsdp', 'group')), may hold values from 0.04 to 600
Outputs:
- updates: bfloat16 [32, 512, 512], P('group', 'fsdp')
Inputs may be any that keep to these rules, and one draw needn't show every extreme that they name: Each row of owners is a permutation of the 8 indices along fsdp. `left_factors`: each block is symmetric and positive definite. `right_factors`: each block is symmetric and positive definite.
All inputs are finite; a program needn't handle non-finite values.
Results may differ from a plain program's by a relative error of at most 0.01.
Values may be sent and summed in bfloat16 or wider, within the bound.
A program may use at most 64 MiB of HBM per device.

v0:
```python
import jax
import jax.numpy as jnp
from jax import lax
from jax.sharding import PartitionSpec as P

factor_decay = 0.95
moment_decay = 0.95
epsilon = 1e-08
clip_rms = 0.25


def refresh(factor, old_basis):
    projected = jnp.dot(factor, old_basis, precision=lax.Precision.HIGHEST)
    correlation = jnp.dot(projected.T, projected, precision=lax.Precision.HIGHEST)
    cholesky_factor = jnp.linalg.cholesky(correlation)
    solved = jax.scipy.linalg.solve_triangular(cholesky_factor, projected.T, lower=True)
    return solved.T.astype(jnp.bfloat16)


def on_device(gradients, owners, left_factors, right_factors, left_bases, right_bases, moments):
    fsdp_count = lax.axis_size("fsdp")
    owner_row = owners[0]
    positions = jnp.arange(fsdp_count, dtype=jnp.int32)
    matches = owner_row[:, None] == positions[None, :]
    inverse = jnp.sum(jnp.where(matches, positions[:, None], 0), axis=0)
    outgoing = jnp.take(gradients, inverse, axis=0)
    gathered = lax.all_to_all(outgoing, "fsdp", split_axis=0, concat_axis=1, tiled=True)
    gradient = gathered[0]
    width = gradient.shape[0]
    left_gram = jnp.dot(gradient, gradient.T, preferred_element_type=jnp.float32)
    right_gram = jnp.dot(gradient.T, gradient, preferred_element_type=jnp.float32)
    left_new = factor_decay * left_factors[0] + (1.0 - factor_decay) * left_gram
    right_new = factor_decay * right_factors[0] + (1.0 - factor_decay) * right_gram
    left_rotate = refresh(left_new, left_bases[0])
    right_rotate = refresh(right_new, right_bases[0])
    first = jnp.dot(left_rotate.T, gradient, preferred_element_type=jnp.float32).astype(
        jnp.bfloat16
    )
    rotated = jnp.dot(first, right_rotate, preferred_element_type=jnp.float32)
    moment_new = moment_decay * moments[0] + (1.0 - moment_decay) * rotated * rotated
    normed_full = rotated / (jnp.sqrt(moment_new) + epsilon)
    normed = normed_full.astype(jnp.bfloat16)
    back = jnp.dot(left_rotate, normed, preferred_element_type=jnp.float32).astype(jnp.bfloat16)
    unclipped = jnp.dot(back, right_rotate.T, preferred_element_type=jnp.float32)
    squares = jnp.sum(unclipped * unclipped)
    count = jnp.asarray(fsdp_count * lax.axis_size("group") * width * width, jnp.float32)
    pieces = lax.all_to_all(
        unclipped[None].astype(jnp.bfloat16), "fsdp", split_axis=1, concat_axis=0, tiled=True
    ).astype(jnp.float32)
    total = lax.psum(squares, ("fsdp", "group"))
    scale = jnp.minimum(1.0, clip_rms * jnp.sqrt(count) / jnp.sqrt(total + 1e-06))
    return (scale * jnp.take(pieces, owner_row, axis=0)).astype(jnp.bfloat16)


def solution(mesh):
    in_specs = (
        P("group", "fsdp", None),
        P("group", None),
        P(("fsdp", "group"), None, None),
        P(("fsdp", "group"), None, None),
        P(("fsdp", "group"), None, None),
        P(("fsdp", "group"), None, None),
        P(("fsdp", "group"), None, None),
    )
    out_specs = P("group", "fsdp", None)
    return jax.shard_map(
        on_device, mesh=mesh, in_specs=in_specs, out_specs=out_specs, check_vma=False
    )
```

profile of v0, /device:TPU:0, one launch (start us, length us, event | category | flops | bytes accessed | tf_op | source)
XLA Modules:
  0.0 415.2 jit_solution(13667113970826376778)
XLA Ops:
  0.9 1.6 gather_fusion
  3.4 5.2 %all-to-all-start = ((bf16[8,64,512]{2,1,0:T(8,128)(2,1)}), bf16[8,64,512]{2,1,0:T(8,128)(2,1)S(1)}, u32[]{:S(2)}, u32[]{:S(2)}) async-start(bf16[8,64,512]{2,1,0:T(8,128)(2,1)} %broadcast_select_fusion), calls=%async_computation | async-start | bytes 1048576 | tf_op jit(solution)/shard_map/all_to_all | solution.py:27
  8.6 9.7 %all-to-all-done = bf16[8,64,512]{2,1,0:T(8,128)(2,1)S(1)} async-done(((bf16[8,64,512]{2,1,0:T(8,128)(2,1)}), bf16[8,64,512]{2,1,0:T(8,128)(2,1)S(1)}, u32[]{:S(2)}, u32[]{:S(2)}) %all-to-all-start) | async-done | bytes 524320 | tf_op jit(solution)/shard_map/all_to_all | solution.py:27
  19.6 1.8 fusion.14
  21.5 1.9 fusion.78
  24.7 1.4 fusion.13
  27.1 11.7 %cholesky.286 = f32[128,128]{1,0:T(8,128)S(1)} custom-call(f32[128,128]{1,0:T(8,128)S(1)} %cholesky.426), custom_call_target="Cholesky" | custom-call | tf_op jit(solution)/shard_map/jit(cholesky)/cholesky | solution.py:15
  38.9 9.8 %custom-call.27 = f32[1,128,128]{1,2,0:T(8,128)S(1)} custom-call(f32[1,128,128]{2,1,0:T(8,128)S(1)} %get-tuple-element.54), custom_call_target="InvertDiagBlocksLowerTriangular" | custom-call | tf_op jit(solution)/shard_map/jit(cholesky)/cholesky | solution.py:15
  51.3 12.0 %cholesky.305 = f32[128,128]{1,0:T(8,128)S(1)} custom-call(f32[128,128]{1,0:T(8,128)S(1)} %cholesky.430), custom_call_target="Cholesky" | custom-call | tf_op jit(solution)/shard_map/jit(cholesky)/cholesky | solution.py:15
  63.3 9.8 %custom-call.28 = f32[1,128,128]{1,2,0:T(8,128)S(1)} custom-call(f32[1,128,128]{2,1,0:T(8,128)S(1)} %get-tuple-element.51), custom_call_target="InvertDiagBlocksLowerTriangular" | custom-call | tf_op jit(solution)/shard_map/jit(cholesky)/cholesky | solution.py:15
  74.7 11.7 %cholesky.326 = f32[128,128]{1,0:T(8,128)S(1)} custom-call(f32[128,128]{1,0:T(8,128)S(1)} %cholesky.435), custom_call_target="Cholesky" | custom-call | tf_op jit(solution)/shard_map/jit(cholesky)/cholesky | solution.py:15
  88.5 9.8 %custom-call.29 = f32[1,128,128]{1,2,0:T(8,128)S(1)} custom-call(f32[1,128,128]{2,1,0:T(8,128)S(1)} %get-tuple-element.48), custom_call_target="InvertDiagBlocksLowerTriangular" | custom-call | tf_op jit(solution)/shard_map/jit(cholesky)/cholesky | solution.py:15
  98.5 14.0 %convolution_subtract_fusion.11 = f32[128,128]{1,0:T(8,128)S(1)} fusion(f32[512,512]{1,0:T(8,128)S(1)} %convolution_dynamic-update-slice_fusion.3, f32[512,512]{1,0:T(8,128)} %copy-done.4), kind=kOutput, calls=%fused_computation.33 | convolution fusion | flops 75513856 | bytes 327680 | tf_op jit(solution)/shard_map/jit(cholesky)/cholesky | solution.py:15
  112.5 11.7 %cholesky.343 = f32[128,128]{1,0:T(8,128)S(1)} custom-call(f32[128,128]{1,0:T(8,128)S(1)} %convolution_subtract_fusion.11), custom_call_target="Cholesky" | custom-call | tf_op jit(solution)/shard_map/jit(cholesky)/cholesky | solution.py:15
  128.4 11.2 %while.4 = (s32[]{:T(128)}, f32[512,512]{1,0:T(8,128)}, s32[4,2]{0,1:T(2,128)S(1)}, f32[4,128,128]{2,1,0:T(8,128)S(1)}, s32[]{:T(128)}) while((s32[]{:T(128)}, f32[512,512]{1,0:T(8,128)}, s32[4,2]{0,1:T(2,128)S(1)}, f32[4,128,128]{2,1,0:T(8,128)S(1)}, s32[]{:T(128)}) %tuple.56), condition=%wide.while_cond, body=%wide.while_body.sunk | while | flops 2 | bytes 131181 | solution.py:16
  129.0 2.2 bitcast_dynamic-update-slice_fusion.4
  131.8 2.2 bitcast_dynamic-update-slice_fusion.4
  134.6 2.2 bitcast_dynamic-update-slice_fusion.4
  137.5 2.1 bitcast_dynamic-update-slice_fusion.4
  139.6 39.3 %custom-call.30 = f32[4,128,128]{1,2,0:T(8,128)S(1)} custom-call(f32[4,128,128]{2,1,0:T(8,128)S(1)} %get-tuple-element.21), custom_call_target="InvertDiagBlocksLowerTriangular" | custom-call | tf_op jit(solution)/shard_map/jit(_solve_triangular)/triangular_solve | solution.py:16
  179.4 1.4 convolution_subtract_fusion.3
  181.2 2.0 convolution_subtract_fusion.2
  183.7 2.5 convolution_subtract_fusion.5
  188.5 1.8 fusion.11
  190.4 1.9 fusion.79
  193.6 1.4 fusion.10
  196.0 12.1 %cholesky.358 = f32[128,128]{1,0:T(8,128)S(1)} custom-call(f32[128,128]{1,0:T(8,128)S(1)} %cholesky.439), custom_call_target="Cholesky" | custom-call | tf_op jit(solution)/shard_map/jit(cholesky)/cholesky | solution.py:15
  208.2 9.8 %custom-call.31 = f32[1,128,128]{1,2,0:T(8,128)S(1)} custom-call(f32[1,128,128]{2,1,0:T(8,128)S(1)} %get-tuple-element.64), custom_call_target="InvertDiagBlocksLowerTriangular" | custom-call | tf_op jit(solution)/shard_map/jit(cholesky)/cholesky | solution.py:15
  221.3 11.7 %cholesky.377 = f32[128,128]{1,0:T(8,128)S(1)} custom-call(f32[128,128]{1,0:T(8,128)S(1)} %cholesky.443), custom_call_target="Cholesky" | custom-call | tf_op jit(solution)/shard_map/jit(cholesky)/cholesky | solution.py:15
  233.6 9.8 %custom-call.32 = f32[1,128,128]{1,2,0:T(8,128)S(1)} custom-call(f32[1,128,128]{2,1,0:T(8,128)S(1)} %get-tuple-element.61), custom_call_target="InvertDiagBlocksLowerTriangular" | custom-call | tf_op jit(solution)/shard_map/jit(cholesky)/cholesky | solution.py:15
  246.5 13.3 %cholesky.398 = f32[128,128]{1,0:T(8,128)} custom-call(f32[128,128]{1,0:T(8,128)} %cholesky.448), custom_call_target="Cholesky" | custom-call | tf_op jit(solution)/shard_map/jit(cholesky)/cholesky | solution.py:15
  259.8 1.5 select_reduce_fusion.1
  264.0 11.3 %custom-call.33 = f32[1,128,128]{1,2,0:T(8,128)} custom-call(f32[1,128,128]{2,1,0:T(8,128)} %get-tuple-element.58), custom_call_target="InvertDiagBlocksLowerTriangular" | custom-call | tf_op jit(solution)/shard_map/jit(cholesky)/cholesky | solution.py:15
  277.5 11.7 %cholesky.415 = f32[128,128]{1,0:T(8,128)S(1)} custom-call(f32[128,128]{1,0:T(8,128)S(1)} %convolution_subtract_fusion.10), custom_call_target="Cholesky" | custom-call | tf_op jit(solution)/shard_map/jit(cholesky)/cholesky | solution.py:15
  293.6 11.6 %while.5 = (s32[]{:T(128)}, f32[512,512]{1,0:T(8,128)}, s32[4,2]{0,1:T(2,128)S(1)}, f32[4,128,128]{2,1,0:T(8,128)S(1)}, s32[]{:T(128)}) while((s32[]{:T(128)}, f32[512,512]{1,0:T(8,128)}, s32[4,2]{0,1:T(2,128)S(1)}, f32[4,128,128]{2,1,0:T(8,128)S(1)}, s32[]{:T(128)}) %tuple.59), condition=%wide.while_cond.clone, body=%wide.while_body.clone.sunk | while | flops 2 | bytes 131181 | solution.py:16
  294.2 2.2 bitcast_dynamic-update-slice_fusion.5
  297.2 2.2 bitcast_dynamic-update-slice_fusion.5
  300.1 2.2 bitcast_dynamic-update-slice_fusion.5
  303.0 2.2 bitcast_dynamic-update-slice_fusion.5
  305.2 39.5 %custom-call.34 = f32[4,128,128]{1,2,0:T(8,128)S(1)} custom-call(f32[4,128,128]{2,1,0:T(8,128)S(1)} %get-tuple-element.22), custom_call_target="InvertDiagBlocksLowerTriangular" | custom-call | tf_op jit(solution)/shard_map/jit(_solve_triangular)/triangular_solve | solution.py:16
  345.2 1.4 convolution_subtract_fusion.1
  347.0 1.9 convolution_subtract_fusion
  349.4 2.5 convolution_subtract_fusion.4
  353.3 3.3 fusion.9
  356.6 2.6 multiply_reduce_fusion
  360.5 3.8 reduce.16
  365.5 3.5 all-to-all-start.1
  369.0 43.1 %psum.7 = f32[]{:T(128)} all-reduce(f32[]{:T(128)} %get-tuple-element.43), channel_id=1, replica_groups=mesh['fsdp'=8,'group'=4] {'fsdp','group'}, use_global_device_ids=true, to_apply=%region_10.13 | all-reduce | flops 1 | bytes 8 | tf_op jit(solution)/shard_map/psum | solution.py:50
  (122 shorter events, 45.7 us)
Async XLA Ops:
  0.0 19.6 %copy-start = (f32[1,512,512]{2,1,0:T(8,128)S(1)}, f32[1,512,512]{2,1,0:T(8,128)}, u32[]{:S(2)}) copy-start(f32[1,512,512]{2,1,0:T(8,128)} %param.14) | copy-start | bytes 3145732
  0.0 0.7 copy-start.17
  2.5 16.6 %copy-start.8 = (f32[1,512,512]{2,1,0:T(8,128)S(1)}, f32[1,512,512]{2,1,0:T(8,128)}, u32[]{:S(2)}) copy-start(f32[1,512,512]{2,1,0:T(8,128)} %param.12) | copy-start | bytes 3145732
  3.4 14.9 %all-to-all-start = ((bf16[8,64,512]{2,1,0:T(8,128)(2,1)}), bf16[8,64,512]{2,1,0:T(8,128)(2,1)S(1)}, u32[]{:S(2)}, u32[]{:S(2)}) async-start(bf16[8,64,512]{2,1,0:T(8,128)(2,1)} %broadcast_select_fusion), calls=%async_computation | async-start | bytes 1048576 | tf_op jit(solution)/shard_map/all_to_all | solution.py:27
  18.3 0.8 copy-start.1
  26.1 1.0 copy-start.4
  181.2 2.4 copy-start.6
  183.7 2.5 copy-start.10
  183.7 3.6 copy-start.2
  183.7 3.6 copy-start.19
  187.3 1.2 copy-start.9
  195.0 1.0 copy-start.5
  220.6 0.7 copy-start.14
  261.9 0.6 copy-start.18
  344.7 4.2 %copy-start.15 = (f32[4,128,128]{1,2,0:T(8,128)}, f32[4,128,128]{1,2,0:T(8,128)S(1)}, u32[]{:S(2)}) copy-start(f32[4,128,128]{1,2,0:T(8,128)S(1)} %custom-call.34) | copy-start | bytes 786436
  349.4 2.5 copy-start.12
  349.4 3.9 copy-start.3
  351.9 1.3 copy-start.7
  351.9 1.3 copy-start.16
  353.3 3.3 copy-start.11
  353.3 3.3 copy-start.13
  365.5 47.2 %all-to-all-start.1 = ((bf16[8,2,16384]{2,1,0:T(2,128)(2,1)}), bf16[8,2,16384]{2,1,0:T(2,128)(2,1)S(1)}, u32[]{:S(2)}, u32[]{:S(2)}) async-start(bf16[8,2,16384]{2,1,0:T(2,128)(2,1)} %reshape.140), calls=%async_computation.1 | async-start | bytes 1048576 | tf_op jit(solution)/shard_map/all_to_all | solution.py:47
where the time goes:
time: 419 us; the launch traced here: 415 us
  other arithmetic  254 us (61%)
  matrix products  56.3 us (13%)
  blocking collectives  43.1 us (10%)
  local copies, waits for them, and re-layouts  37.3 us (9%)
  waiting for transfers between devices  9.74 us (2%)
  starting transfers between devices  8.66 us (2%)
  between operations  6.4 us (2%)
    another operation x30, other arithmetic, refresh(): cholesky_factor = jnp.linalg.cholesky(correlation)  164 us
    another operation x5, other arithmetic, refresh(): jax.scipy.linalg.solve_triangular(cholesky_factor, projected.T, lower=True)  81.1 us
    psum x1, blocking collectives, on_device(): total = lax.psum(squares, ('fsdp', 'group'))  43.1 us
    another operation x12, matrix products, refresh(): cholesky_factor = jnp.linalg.cholesky(correlation)  25.4 us
    another operation x27, local copies, waits for them, and re-layouts, refresh(): jax.scipy.linalg.solve_triangular(cholesky_factor, projected.T, lower=True)  22.7 us
    another operation x14, matrix products, refresh(): jax.scipy.linalg.solve_triangular(cholesky_factor, projected.T, lower=True)  16.6 us
    all_to_all x1, waiting for transfers between devices, on_device(): lax.all_to_all(outgoing, 'fsdp', split_axis=0, concat_axis=1, tiled=True)  9.74 us
  transfers between devices with their start and end apart: 2, of which 1 were waited for; matrix products, arithmetic and copies ran while one was open for 0% of the time, Pallas kernels for 0%

commit v1 on v0

v1 whole, which is shorter than its diff:
```python
import functools

import jax
import jax.numpy as jnp
from jax import lax
from jax.experimental import pallas as pl
from jax.experimental.pallas import tpu as pltpu
from jax.sharding import PartitionSpec as P

factor_decay = 0.95
moment_decay = 0.95
epsilon = 1e-08
clip_rms = 0.25

panel = 128
tile = 8
NN = (((1,), (0,)), ((), ()))
NT = (((1,), (1,)), ((), ()))
TN = (((0,), (0,)), ((), ()))


def mm(a, b, dims):
    return lax.dot_general(a, b, dims, preferred_element_type=jnp.float32)


def split(x):
    high = x.astype(jnp.bfloat16)
    low = (x - high.astype(jnp.float32)).astype(jnp.bfloat16)
    return high, low


def mm3(a, b, dims):
    (ah, al), (bh, bl) = a, b
    return mm(ah, bh, dims) + (mm(ah, bl, dims) + mm(al, bh, dims))


def gram(x):
    return lax.dot_general(
        x, x, NT, precision=lax.Precision.HIGHEST, preferred_element_type=jnp.float32
    )


def lane_copy(x, at):
    return jnp.broadcast_to(x[:, at : at + 1], x.shape)


def row_copy(x, at):
    return jnp.broadcast_to(x[at : at + 1, :], x.shape)


def reciprocal(x):
    guess = pl.reciprocal(x, approx=True)
    guess = guess * (2.0 - x * guess)
    return guess * (2.0 - x * guess)


def root_reciprocal(x):
    guess = lax.rsqrt(x)
    return guess * (1.5 - 0.5 * x * guess * guess)


def pivot_rows(first, own, columns):
    row_id = lax.broadcasted_iota(jnp.int32, own.shape, 0)
    lane_id = lax.broadcasted_iota(jnp.int32, own.shape, 1) - first
    inside = (lane_id >= 0) & (lane_id < tile)
    solved = jnp.where(inside, jnp.where(lane_id == row_id, 1.0, 0.0), own)
    factored = solved
    columns = list(columns)
    for j in range(0, tile, 2):
        left, right = columns[j], columns[j + 1]
        a, b, c = row_copy(left, j), row_copy(left, j + 1), row_copy(right, j + 1)
        det = a * c - b * b
        inv = reciprocal(det)
        ia, ib, ic = c * inv, b * inv, a * inv
        root = root_reciprocal(a)
        tail = root_reciprocal(det * root * root)
        is_first, is_second = row_id == j, row_id == j + 1

        def eliminate(x):
            upper, lower = row_copy(x, j), row_copy(x, j + 1)
            new_upper = ia * upper - ib * lower
            new_lower = ic * lower - ib * upper
            rest = x - left * new_upper - right * new_lower
            new = jnp.where(is_first, new_upper, jnp.where(is_second, new_lower, rest))
            return new, upper, lower

        for l in range(j + 2, tile):
            columns[l] = eliminate(columns[l])[0]
        solved, upper, lower = eliminate(solved)
        y_upper = upper * root
        y_lower = (lower - b * root * y_upper) * tail
        factored = jnp.where(is_first, y_upper, jnp.where(is_second, y_lower, factored))
    return solved, factored


def inverse_cholesky(matrices):
    count = panel // tile
    rows = [[m[g * tile : (g + 1) * tile, :] for g in range(count)] for m in matrices]
    done = [[None] * count for _ in matrices]
    lane_id = lax.broadcasted_iota(jnp.int32, (tile, panel), 1)
    for p in range(count):
        first = p * tile
        inside = (lane_id >= first) & (lane_id < first + tile)
        for m, groups in enumerate(rows):
            columns = [lane_copy(groups[p], first + j) for j in range(tile)]
            solved, factored = pivot_rows(first, groups[p], columns)
            done[m][p] = jnp.where(lane_id < first + tile, factored, 0.0)
            if p + 1 < count:
                solved_rows = [row_copy(solved, j) for j in range(tile)]
                for g in range(p + 1, count):
                    old = groups[g]
                    new = jnp.where(inside, 0.0, old)
                    for j in range(tile):
                        new = new - lane_copy(old, first + j) * solved_rows[j]
                    groups[g] = new
    return [jnp.concatenate(d, axis=0) for d in done]


def refresh(projected, high, low, panels):
    for side in range(2):
        high[side] = jnp.zeros_like(high[side])
        low[side] = jnp.zeros_like(low[side])

    def step(k, carry):
        rows = pl.ds(pl.multiple_of(k * panel, panel), panel)
        blocks = []
        for side in range(2):
            block = projected[side, rows, :]
            basis = (high[side], low[side])
            inner = mm3(split(block), basis, NT)
            block = block - mm3(split(inner), basis, NN)
            block = block * lax.rsqrt(jnp.sum(block * block, axis=1, keepdims=True))
            blocks.append(block)
        inverses = inverse_cholesky([gram(b) for b in blocks])
        for side in range(2):
            q = mm3(split(inverses[side]), split(blocks[side]), NN)
            qh, ql = split(q)
            high[side, rows, :] = qh
            low[side, rows, :] = ql
        return carry

    lax.fori_loop(0, panels, step, 0)


def local_kernel(
    g_ref, l_ref, r_ref, ql_ref, qr_ref, v_ref, u_ref, s_ref, projected, high, low
):
    width = g_ref.shape[0]
    g = g_ref[...]
    left = factor_decay * l_ref[0] + (1.0 - factor_decay) * mm(g, g, NT)
    projected[0] = mm3(split(ql_ref[0]), split(left), TN)
    right = factor_decay * r_ref[0] + (1.0 - factor_decay) * mm(g, g, TN)
    projected[1] = mm3(split(qr_ref[0]), split(right), TN)
    refresh(projected, high, low, width // panel)
    first = mm(high[0], g, NN).astype(jnp.bfloat16)
    rotated = mm(first, high[1], NT)
    moment = moment_decay * v_ref[0] + (1.0 - moment_decay) * rotated * rotated
    normed = (rotated / (jnp.sqrt(moment) + epsilon)).astype(jnp.bfloat16)
    back = mm(high[0], normed, TN).astype(jnp.bfloat16)
    update = mm(back, high[1], NN)
    u_ref[...] = update.astype(jnp.bfloat16)
    s_ref[...] = jnp.sum(update * update, axis=0, keepdims=True)


def local(gradient, *states):
    width = gradient.shape[0]
    vmem = pl.BlockSpec(memory_space=pltpu.VMEM)
    return pl.pallas_call(
        local_kernel,
        out_shape=(
            jax.ShapeDtypeStruct((width, width), jnp.bfloat16),
            jax.ShapeDtypeStruct((1, width), jnp.float32),
        ),
        in_specs=[vmem] * 6,
        out_specs=(vmem, vmem),
        scratch_shapes=[
            pltpu.VMEM((2, width, width), jnp.float32),
            pltpu.VMEM((2, width, width), jnp.bfloat16),
            pltpu.VMEM((2, width, width), jnp.bfloat16),
        ],
        compiler_params=pltpu.CompilerParams(vmem_limit_bytes=48 * 1024 * 1024),
        name="local_update",
    )(gradient, *states)


def on_device(gradients, owners, left_factors, right_factors, left_bases, right_bases, moments):
    fsdp_count = lax.axis_size("fsdp")
    owner_row = owners[0]
    positions = jnp.arange(fsdp_count, dtype=jnp.int32)
    matches = owner_row[:, None] == positions[None, :]
    inverse = jnp.sum(jnp.where(matches, positions[:, None], 0), axis=0)
    outgoing = jnp.take(gradients, inverse, axis=0)
    gathered = lax.all_to_all(outgoing, "fsdp", split_axis=0, concat_axis=1, tiled=True)
    gradient = gathered[0]
    width = gradient.shape[0]
    unclipped, sums = local(
        gradient, left_factors, right_factors, left_bases, right_bases, moments
    )
    squares = jnp.sum(sums)
    count = jnp.asarray(fsdp_count * lax.axis_size("group") * width * width, jnp.float32)
    pieces = lax.all_to_all(
        unclipped[None], "fsdp", split_axis=1, concat_axis=0, tiled=True
    ).astype(jnp.float32)
    total = lax.psum(squares, ("fsdp", "group"))
    scale = jnp.minimum(1.0, clip_rms * jnp.sqrt(count) / jnp.sqrt(total + 1e-06))
    return (scale * jnp.take(pieces, owner_row, axis=0)).astype(jnp.bfloat16)


def solution(mesh):
    in_specs = (
        P("group", "fsdp", None),
        P("group", None),
        P(("fsdp", "group"), None, None),
        P(("fsdp", "group"), None, None),
        P(("fsdp", "group"), None, None),
        P(("fsdp", "group"), None, None),
        P(("fsdp", "group"), None, None),
    )
    out_specs = P("group", "fsdp", None)
    return jax.shard_map(
        on_device, mesh=mesh, in_specs=in_specs, out_specs=out_specs, check_vma=False
    )
```

time: 419 us -> 117 us (0.28)
  other arithmetic: 254 us -> 5.73 us
  matrix products: 56.3 us -> 0 us
  Pallas kernels: 0 us -> 43.1 us
  local copies, waits for them, and re-layouts: 37.3 us -> 6.5 us
  blocking collectives: 43.1 us -> 57.2 us
  waiting for transfers between devices: 9.74 us -> 0.01 us
  between operations: 6.4 us -> 0.87 us
  starting transfers between devices: 8.66 us -> 3.49 us
    another operation x35 -> x0, other arithmetic: 245 us -> none  [the longest x30 164 us: refresh(): cholesky_factor = jnp.linalg.cholesky(correlation)]
    pallas_call x0 -> x1, Pallas kernels: none -> 43.1 us  [local(): pl.pallas_call(local_kernel, out_shape=(jax.ShapeDtypeStruct((width, widt...]
    another operation x26 -> x0, matrix products: 42.1 us -> none  [the longest x12 25.4 us: refresh(): cholesky_factor = jnp.linalg.cholesky(correlation)]
    another operation x35 -> x0, local copies, waits for them, and re-layouts: 23.6 us -> none  [the longest x27 22.7 us: refresh(): jax.scipy.linalg.solve_triangular(cholesky_factor, projected.T, lower=True)]
    all_to_all x0 -> x1, blocking collectives: none -> 14.8 us  [on_device(): lax.all_to_all(outgoing, 'fsdp', split_axis=0, concat_axis=1, tiled=True)]
    dot_general x8 -> x0, matrix products: 14.3 us -> none  [the longest x2 3.71 us: refresh(): jnp.dot(projected.T, projected, precision=lax.Precision.HIGHEST)]
    all_to_all x2 -> x1, waiting for transfers between devices: 9.74 us -> 0.01 us  [on_device(): lax.all_to_all(unclipped[None], 'fsdp', split_axis=1, concat_axis=0, tile...]
    all_to_all x2 -> x1, starting transfers between devices: 8.66 us -> 3.49 us  [on_device(): lax.all_to_all(unclipped[None], 'fsdp', split_axis=1, concat_axis=0, tile...]
  transfers between devices with their start and end apart: 2 -> 1, of which waited for: 1 -> 0; matrix products, arithmetic and copies ran while one was open for 0% -> 1% of each run, Pallas kernels for 0% -> 0%
where the time goes in v1:
time: 117 us
  blocking collectives  57.2 us (49%)
  Pallas kernels  43.1 us (37%)
  local copies, waits for them, and re-layouts  6.5 us (6%)
  other arithmetic  5.73 us (5%)
  starting transfers between devices  3.49 us (3%)
    pallas_call x1, Pallas kernels, local(): pl.pallas_call(local_kernel, out_shape=(jax.ShapeDtypeStruct((width, widt...  43.1 us
    psum x1, blocking collectives, on_device(): total = lax.psum(squares, ('fsdp', 'group'))  42.4 us
    all_to_all x1, blocking collectives, on_device(): lax.all_to_all(outgoing, 'fsdp', split_axis=0, concat_axis=1, tiled=True)  14.8 us
    unnamed x16, local copies, waits for them, and re-layouts  4.49 us
    unnamed x1, other arithmetic  3.82 us
    all_to_all x1, starting transfers between devices, on_device(): lax.all_to_all(unclipped[None], 'fsdp', split_axis=1, concat_axis=0, tile...  3.49 us
  transfers between devices with their start and end apart: 1, of which 0 were waited for; matrix products, arithmetic and copies ran while one was open for 1% of the time, Pallas kernels for 0%

profile of v1, /device:TPU:0, one launch (start us, length us, event | category | flops | bytes accessed | tf_op | source)
XLA Modules:
  0.0 116.9 jit_solution(4431166845268452297)
XLA Ops:
  0.0 0.0 copy-start
  0.0 0.0 copy-start.5
  0.0 0.7 copy-done.5
  0.7 0.1 select_reduce_fusion
  0.8 0.2 copy-done
  1.1 0.0 copy-start.3
  1.1 0.6 gather_fusion
  1.6 0.0 copy-start.1
  1.7 0.0 copy-start.2
  1.7 0.1 broadcast_select_fusion
  1.8 14.8 %all_to_all.8 = bf16[8,64,512]{2,1,0:T(8,128)(2,1)S(1)} all-to-all(bf16[8,64,512]{2,1,0:T(8,128)(2,1)S(1)} %broadcast_select_fusion), channel_id=1, replica_groups=mesh['fsdp'=8,'group'=4] {'fsdp'}, dimensions={0} | all-to-all | bytes 1048576 | tf_op jit(solution)/shard_map/all_to_all | solution.py:193
  16.6 0.0 copy-done.3
  16.6 0.0 copy-done.1
  16.6 0.0 copy-done.2
  16.6 0.0 copy-start.4
  16.7 1.2 %copy-done.4 = f32[1,512,512]{2,1,0:T(8,128)S(1)} copy-done((f32[1,512,512]{2,1,0:T(8,128)S(1)}, f32[1,512,512]{2,1,0:T(8,128)}, u32[]{:S(2)}) %copy-start.4) | copy-done | bytes 1048600
  17.9 43.1 %local_update.1 = (bf16[512,512]{1,0:T(8,128)(2,1)S(1)}, f32[1,512]{1,0:T(1,128)S(1)}) custom-call(bf16[512,512]{1,0:T(8,128)(2,1)S(1)} %bitcast.17, f32[1,512,512]{2,1,0:T(8,128)S(1)} %copy-done.1, f32[1,512,512]{2,1,0:T(8,128)S(1)} %copy-done.2, f32[1,512,512]{2,1,0:T(8,128)S(1)} %copy-done.3, f32[1,512,512]{2,1,0:T(8,128)S(1)} %copy-done.4, ...), custom_call_target="tpu_custom_call" | custom-call | tf_op jit(solution)/shard_map/local_update/pallas_call | solution.py:168
  61.0 0.8 copy.12
  61.8 0.5 broadcast.72
  62.3 3.8 %reduce = bf16[512,512]{1,0:T(8,128)(2,1)S(1)} reduce(bf16[512,1,512]{2,1,0:T(2,128)(2,1)S(1)} %bitcast.20, bf16[]{:T(256)} %broadcast.72), dimensions={1}, to_apply=%bitcast.16.reduce_sub_computation | reduce | bytes 1048578
  66.1 1.2 reshape.79
  67.3 3.5 %all-to-all-start.1 = ((bf16[8,2,16384]{2,1,0:T(2,128)(2,1)}), bf16[8,2,16384]{2,1,0:T(2,128)(2,1)S(1)}, u32[]{:S(2)}, u32[]{:S(2)}) async-start(bf16[8,2,16384]{2,1,0:T(2,128)(2,1)} %reshape.79), calls=%async_computation.1 | async-start | bytes 1048576 | tf_op jit(solution)/shard_map/all_to_all | solution.py:201
  70.8 0.7 reduce_sum.22
  71.5 42.4 %psum.7 = f32[]{:T(128)} all-reduce(f32[]{:T(128)} %reduce_sum.22), channel_id=1, replica_groups=mesh['fsdp'=8,'group'=4] {'fsdp','group'}, use_global_device_ids=true, to_apply=%region_2.3 | all-reduce | flops 1 | bytes 8 | tf_op jit(solution)/shard_map/psum | solution.py:204
  114.7 0.0 all-to-all-done.1
  114.7 0.5 reshape.80
  115.2 0.1 copy.10
  115.3 0.6 gather_fusion.1
  115.9 1.0 multiply_convert_fusion
  (6 shorter events, 0.0 us)
Async XLA Ops:
  0.0 1.1 copy-start
  0.0 0.7 copy-start.5
  1.1 15.6 %copy-start.3 = (f32[1,512,512]{2,1,0:T(8,128)S(1)}, f32[1,512,512]{2,1,0:T(8,128)}, u32[]{:S(2)}) copy-start(f32[1,512,512]{2,1,0:T(8,128)} %ql_ref.1) | copy-start | bytes 3145732
  1.6 15.0 %copy-start.1 = (f32[1,512,512]{2,1,0:T(8,128)S(1)}, f32[1,512,512]{2,1,0:T(8,128)}, u32[]{:S(2)}) copy-start(f32[1,512,512]{2,1,0:T(8,128)} %l_ref.1) | copy-start | bytes 3145732
  1.7 15.0 %copy-start.2 = (f32[1,512,512]{2,1,0:T(8,128)S(1)}, f32[1,512,512]{2,1,0:T(8,128)}, u32[]{:S(2)}) copy-start(f32[1,512,512]{2,1,0:T(8,128)} %r_ref.1) | copy-start | bytes 3145732
  16.6 1.2 %copy-start.4 = (f32[1,512,512]{2,1,0:T(8,128)S(1)}, f32[1,512,512]{2,1,0:T(8,128)}, u32[]{:S(2)}) copy-start(f32[1,512,512]{2,1,0:T(8,128)} %qr_ref.1) | copy-start | bytes 3145732
  67.3 47.4 %all-to-all-start.1 = ((bf16[8,2,16384]{2,1,0:T(2,128)(2,1)}), bf16[8,2,16384]{2,1,0:T(2,128)(2,1)S(1)}, u32[]{:S(2)}, u32[]{:S(2)}) async-start(bf16[8,2,16384]{2,1,0:T(2,128)(2,1)} %reshape.79), calls=%async_computation.1 | async-start | bytes 1048576 | tf_op jit(solution)/shard_map/all_to_all | solution.py:201

commit v2 on v1

--- a/solution.py
+++ b/solution.py
@@ -50,7 +50,6 @@
 
 def reciprocal(x):
     guess = pl.reciprocal(x, approx=True)
-    guess = guess * (2.0 - x * guess)
     return guess * (2.0 - x * guess)
 
 
@@ -109,26 +108,32 @@
                 solved_rows = [row_copy(solved, j) for j in range(tile)]
                 for g in range(p + 1, count):
                     old = groups[g]
-                    new = jnp.where(inside, 0.0, old)
-                    for j in range(tile):
-                        new = new - lane_copy(old, first + j) * solved_rows[j]
-                    groups[g] = new
+                    terms = [lane_copy(old, first + j) * solved_rows[j] for j in range(tile)]
+                    while len(terms) > 1:
+                        terms = [x + y for x, y in zip(terms[::2], terms[1::2])]
+                    groups[g] = jnp.where(inside, 0.0, old) - terms[0]
     return [jnp.concatenate(d, axis=0) for d in done]
 
 
+def project_out(side, first, projected, basis_high, basis_low):
+    rest = projected[side, first:, :]
+    rest_high, rest_low = split(rest)
+    both = jnp.concatenate([basis_high, basis_low], axis=0)
+    wide = mm(rest_high, both, NT)
+    inner = wide[:, :panel] + (wide[:, panel:] + mm(rest_low, basis_high, NT))
+    inner_high, inner_low = split(inner)
+    twice = jnp.concatenate([basis_high, basis_high], axis=0)
+    split_inner = jnp.concatenate([inner_high, inner_low], axis=1)
+    part = mm(split_inner, twice, NN) + mm(inner_high, basis_low, NN)
+    projected[side, first:, :] = rest - part
+
+
 def refresh(projected, high, low, panels):
-    for side in range(2):
-        high[side] = jnp.zeros_like(high[side])
-        low[side] = jnp.zeros_like(low[side])
-
     def step(k, carry):
         rows = pl.ds(pl.multiple_of(k * panel, panel), panel)
         blocks = []
         for side in range(2):
             block = projected[side, rows, :]
-            basis = (high[side], low[side])
-            inner = mm3(split(block), basis, NT)
-            block = block - mm3(split(inner), basis, NN)
             block = block * lax.rsqrt(jnp.sum(block * block, axis=1, keepdims=True))
             blocks.append(block)
         inverses = inverse_cholesky([gram(b) for b in blocks])
@@ -136,7 +141,15 @@
             q = mm3(split(inverses[side]), split(blocks[side]), NN)
             qh, ql = split(q)
             high[side, rows, :] = qh
-            low[side, rows, :] = ql
+            low[side] = ql
+        for at in range(panels - 1):
+
+            @pl.when(k == at)
+            def _():
+                for side in range(2):
+                    own = high[side, at * panel : (at + 1) * panel, :]
+                    project_out(side, (at + 1) * panel, projected, own, low[side])
+
         return carry
 
     lax.fori_loop(0, panels, step, 0)
@@ -159,7 +172,8 @@
     back = mm(high[0], normed, TN).astype(jnp.bfloat16)
     update = mm(back, high[1], NN)
     u_ref[...] = update.astype(jnp.bfloat16)
-    s_ref[...] = jnp.sum(update * update, axis=0, keepdims=True)
+    squares = jnp.sum((update * update).reshape(width // 8, 8, width), axis=0)
+    s_ref[...] = sum(squares[:, at : at + 128] for at in range(0, width, 128))
 
 
 def local(gradient, *states):
@@ -169,41 +183,192 @@
         local_kernel,
         out_shape=(
             jax.ShapeDtypeStruct((width, width), jnp.bfloat16),
-            jax.ShapeDtypeStruct((1, width), jnp.float32),
+            jax.ShapeDtypeStruct((8, 128), jnp.float32),
         ),
         in_specs=[vmem] * 6,
         out_specs=(vmem, vmem),
         scratch_shapes=[
             pltpu.VMEM((2, width, width), jnp.float32),
             pltpu.VMEM((2, width, width), jnp.bfloat16),
-            pltpu.VMEM((2, width, width), jnp.bfloat16),
+            pltpu.VMEM((2, panel, width), jnp.bfloat16),
         ],
         compiler_params=pltpu.CompilerParams(vmem_limit_bytes=48 * 1024 * 1024),
         name="local_update",
     )(gradient, *states)
 
 
+def position(owners_ref, owner, count):
+    at = 0
+    for j in range(1, count):
+        at = jnp.where(owners_ref[0, j] == owner, j, at)
+    return at
+
+
+def meet(axes):
+    barrier = pltpu.get_barrier_semaphore()
+    others = 0
+    for axis, count in axes:
+        me = lax.axis_index(axis)
+        for d in range(1, count):
+            pl.semaphore_signal(
+                barrier,
+                inc=1,
+                device_id={axis: lax.rem(me + d, count)},
+                device_id_type=pl.DeviceIdType.MESH,
+            )
+            others += 1
+    pl.semaphore_wait(barrier, others)
+
+
+def send(source, target, send_sem, recv_sem, axis, to):
+    copy = pltpu.make_async_remote_copy(
+        src_ref=source,
+        dst_ref=target,
+        send_sem=send_sem,
+        recv_sem=recv_sem,
+        device_id={axis: to},
+        device_id_type=pl.DeviceIdType.MESH,
+    )
+    copy.start()
+    return copy
+
+
+def collect_kernel(count, owners_ref, g_ref, out_ref, outgoing, landing, send_sem, recv_sem):
+    me = lax.axis_index("fsdp")
+    height = g_ref.shape[1]
+    for d in range(1, count):
+        outgoing[d] = g_ref[position(owners_ref, lax.rem(me + d, count), count)]
+    meet([("fsdp", count)])
+    copies = []
+    for d in range(1, count):
+        to = lax.rem(me + d, count)
+        copies.append(
+            send(outgoing.at[d], landing.at[me], send_sem.at[d], recv_sem.at[d], "fsdp", to)
+        )
+    landing[me] = g_ref[position(owners_ref, me, count)]
+    for copy in copies:
+        copy.wait()
+    for f in range(count):
+        out_ref[f * height : (f + 1) * height, :] = landing[f]
+
+
+def collect(owners, gradients, count):
+    _, height, width = gradients.shape
+    return pl.pallas_call(
+        functools.partial(collect_kernel, count),
+        out_shape=jax.ShapeDtypeStruct((count * height, width), gradients.dtype),
+        in_specs=[
+            pl.BlockSpec(memory_space=pltpu.SMEM),
+            pl.BlockSpec(memory_space=pltpu.VMEM),
+        ],
+        out_specs=pl.BlockSpec(memory_space=pltpu.VMEM),
+        scratch_shapes=[
+            pltpu.VMEM((count, height, width), gradients.dtype),
+            pltpu.VMEM((count, height, width), gradients.dtype),
+            pltpu.SemaphoreType.DMA((count,)),
+            pltpu.SemaphoreType.DMA((count,)),
+        ],
+        compiler_params=pltpu.CompilerParams(
+            collective_id=0, has_side_effects=True, vmem_limit_bytes=16 * 1024 * 1024
+        ),
+        name="collect_gradient",
+    )(owners, gradients)
+
+
+def spread_kernel(
+    count,
+    groups,
+    owners_ref,
+    u_ref,
+    s_ref,
+    out_ref,
+    pieces,
+    near,
+    far,
+    mine,
+    piece_send,
+    piece_recv,
+    near_send,
+    near_recv,
+    far_send,
+    far_recv,
+):
+    me, group = lax.axis_index("fsdp"), lax.axis_index("group")
+    height = out_ref.shape[1]
+    meet([("fsdp", count), ("group", groups)])
+    near_copies, piece_copies, far_copies = [], [], []
+    for d in range(1, count):
+        to = lax.rem(me + d, count)
+        near_copies.append(
+            send(s_ref, near.at[me], near_send.at[d], near_recv.at[d], "fsdp", to)
+        )
+    for d in range(1, count):
+        to = lax.rem(me + d, count)
+        rows = pl.ds(pl.multiple_of(to * height, height), height)
+        piece_copies.append(
+            send(u_ref.at[rows], pieces.at[me], piece_send.at[d], piece_recv.at[d], "fsdp", to)
+        )
+    near[me] = s_ref[...]
+    pieces[me] = u_ref[pl.ds(pl.multiple_of(me * height, height), height), :]
+    for copy in near_copies:
+        copy.wait()
+    mine[...] = sum(near[f] for f in range(count))
+    for d in range(1, groups):
+        to = lax.rem(group + d, groups)
+        far_copies.append(
+            send(mine, far.at[group], far_send.at[d], far_recv.at[d], "group", to)
+        )
+    far[group] = mine[...]
+    for copy in far_copies:
+        copy.wait()
+    total = jnp.sum(sum(far[g] for g in range(groups)), axis=1, keepdims=True)
+    total = jnp.sum(total, axis=0, keepdims=True)
+    entries = count * groups * u_ref.shape[0] * u_ref.shape[1]
+    ceiling = clip_rms * entries**0.5
+    scale = jnp.minimum(1.0, ceiling / jnp.sqrt(total + 1e-06))
+    for copy in piece_copies:
+        copy.wait()
+    for j in range(count):
+        piece = pieces[owners_ref[0, j]].astype(jnp.float32)
+        out_ref[j] = (scale * piece).astype(out_ref.dtype)
+
+
+def spread(owners, update, squares, count, groups):
+    width = update.shape[1]
+    height = update.shape[0] // count
+    vmem = pl.BlockSpec(memory_space=pltpu.VMEM)
+    semaphores = pltpu.SemaphoreType.DMA
+    return pl.pallas_call(
+        functools.partial(spread_kernel, count, groups),
+        out_shape=jax.ShapeDtypeStruct((count, height, width), update.dtype),
+        in_specs=[pl.BlockSpec(memory_space=pltpu.SMEM), vmem, vmem],
+        out_specs=vmem,
+        scratch_shapes=[
+            pltpu.VMEM((count, height, width), update.dtype),
+            pltpu.VMEM((count, 8, 128), jnp.float32),
+            pltpu.VMEM((groups, 8, 128), jnp.float32),
+            pltpu.VMEM((8, 128), jnp.float32),
+            semaphores((count,)),
+            semaphores((count,)),
+            semaphores((count,)),
+            semaphores((count,)),
+            semaphores((groups,)),
+            semaphores((groups,)),
+        ],
+        compiler_params=pltpu.CompilerParams(
+            collective_id=1, has_side_effects=True, vmem_limit_bytes=16 * 1024 * 1024
+        ),
+        name="spread_update",
+    )(owners, update, squares)
+
+
 def on_device(gradients, owners, left_factors, right_factors, left_bases, right_bases, moments):
-    fsdp_count = lax.axis_size("fsdp")
-    owner_row = owners[0]
-    positions = jnp.arange(fsdp_count, dtype=jnp.int32)
-    matches = owner_row[:, None] == positions[None, :]
-    inverse = jnp.sum(jnp.where(matches, positions[:, None], 0), axis=0)
-    outgoing = jnp.take(gradients, inverse, axis=0)
-    gathered = lax.all_to_all(outgoing, "fsdp", split_axis=0, concat_axis=1, tiled=True)
-    gradient = gathered[0]
-    width = gradient.shape[0]
-    unclipped, sums = local(
+    count, groups = lax.axis_size("fsdp"), lax.axis_size("group")
+    gradient = collect(owners, gradients, count)
+    update, squares = local(
         gradient, left_factors, right_factors, left_bases, right_bases, moments
     )
-    squares = jnp.sum(sums)
-    count = jnp.asarray(fsdp_count * lax.axis_size("group") * width * width, jnp.float32)
-    pieces = lax.all_to_all(
-        unclipped[None], "fsdp", split_axis=1, concat_axis=0, tiled=True
-    ).astype(jnp.float32)
-    total = lax.psum(squares, ("fsdp", "group"))
-    scale = jnp.minimum(1.0, clip_rms * jnp.sqrt(count) / jnp.sqrt(total + 1e-06))
-    return (scale * jnp.take(pieces, owner_row, axis=0)).astype(jnp.bfloat16)
+    return spread(owners, update, squares, count, groups)
 
 
 def solution(mesh):

time: 117 us -> 67.2 us (0.57)
  blocking collectives: 57.2 us -> 0 us
  Pallas kernels: 43.1 us -> 59.4 us
  other arithmetic: 5.73 us -> 0 us
  starting transfers between devices: 3.49 us -> 0 us
    psum x1 -> x0, blocking collectives: 42.4 us -> none  [on_device(): total = lax.psum(squares, ('fsdp', 'group'))]
    pallas_call x0 -> x2, Pallas kernels: none -> 23.2 us  [the longest x1 12.2 us: spread(): pl.pallas_call(functools.partial(spread_kernel, count, groups), out_shape...]
    all_to_all x1 -> x0, blocking collectives: 14.8 us -> none  [on_device(): lax.all_to_all(outgoing, 'fsdp', split_axis=0, concat_axis=1, tiled=True)]
    pallas_call x1, Pallas kernels: 43.1 us -> 36.2 us  [local(): pl.pallas_call(local_kernel, out_shape=(jax.ShapeDtypeStruct((width, widt...]
    unnamed x1 -> x0, other arithmetic: 3.82 us -> none
    all_to_all x1 -> x0, starting transfers between devices: 3.49 us -> none  [on_device(): lax.all_to_all(unclipped[None], 'fsdp', split_axis=1, concat_axis=0, tile...]
    unnamed x16 -> x15, local copies, waits for them, and re-layouts: 4.49 us -> 6.9 us
    gather x2 -> x0, local copies, waits for them, and re-layouts: 1.19 us -> none  [the longest x1 0.62 us: on_device(): return (scale * jnp.take(pieces, owner_row, axis=0)).astype(jnp.bfloat16)]
  transfers between devices with their start and end apart: 1 -> 0, of which waited for: 0 -> 0; matrix products, arithmetic and copies ran while one was open for 1% -> 0% of each run, Pallas kernels for 0% -> 0%
where the time goes in v2:
time: 67.2 us; the launch traced here: 66.3 us
  Pallas kernels  59.4 us (88%)
  local copies, waits for them, and re-layouts  6.9 us (10%)
    pallas_call x1, Pallas kernels, local(): pl.pallas_call(local_kernel, out_shape=(jax.ShapeDtypeStruct((width, widt...  36.2 us
    pallas_call x1, Pallas kernels, spread(): pl.pallas_call(functools.partial(spread_kernel, count, groups), out_shape...  12.2 us
    pallas_call x1, Pallas kernels, collect(): pl.pallas_call(functools.partial(collect_kernel, count), out_shape=jax.Sh...  11 us
    unnamed x15, local copies, waits for them, and re-layouts  6.9 us

profile of v2, /device:TPU:0, one launch (start us, length us, event | category | flops | bytes accessed | tf_op | source)
XLA Modules:
  0.0 66.3 jit_solution(5776901400214015891)
XLA Ops:
  0.0 0.0 copy-start
  0.0 0.0 copy-start.4
  0.0 1.1 %copy-done.4 = bf16[8,64,512]{2,1,0:T(8,128)(2,1)S(1)} copy-done((bf16[8,64,512]{2,1,0:T(8,128)(2,1)S(1)}, bf16[8,64,512]{2,1,0:T(8,128)(2,1)}, u32[]{:S(2)}) %copy-start.4) | copy-done | bytes 524312
  1.1 0.0 copy-start.5
  1.1 0.7 copy-done.5
  1.8 11.0 %collect_gradient.1.g_ref = bf16[512,512]{1,0:T(8,128)(2,1)S(1)} custom-call(s32[1,8]{1,0:T(1,128)S(1)} %copy-done.5, bf16[8,64,512]{2,1,0:T(8,128)(2,1)S(1)} %copy-done.4), custom_call_target="tpu_custom_call" | custom-call | tf_op jit(solution)/shard_map/collect_gradient/pallas_call | solution.py:257
  12.8 0.0 copy-done
  12.8 0.0 copy-start.1
  12.8 1.2 %copy-done.1 = f32[1,512,512]{2,1,0:T(8,128)S(1)} copy-done((f32[1,512,512]{2,1,0:T(8,128)S(1)}, f32[1,512,512]{2,1,0:T(8,128)}, u32[]{:S(2)}) %copy-start.1) | copy-done | bytes 1048600
  14.0 0.0 copy-start.2
  14.0 1.2 %copy-done.2 = f32[1,512,512]{2,1,0:T(8,128)S(1)} copy-done((f32[1,512,512]{2,1,0:T(8,128)S(1)}, f32[1,512,512]{2,1,0:T(8,128)}, u32[]{:S(2)}) %copy-start.2) | copy-done | bytes 1048600
  15.2 0.0 copy-start.3
  15.2 1.2 %copy-done.3 = f32[1,512,512]{2,1,0:T(8,128)S(1)} copy-done((f32[1,512,512]{2,1,0:T(8,128)S(1)}, f32[1,512,512]{2,1,0:T(8,128)}, u32[]{:S(2)}) %copy-start.3) | copy-done | bytes 1048600
  16.5 36.2 %local_update.1 = (bf16[512,512]{1,0:T(8,128)(2,1)S(1)}, f32[8,128]{1,0:T(8,128)S(1)}) custom-call(bf16[512,512]{1,0:T(8,128)(2,1)S(1)} %collect_gradient.1.g_ref, f32[1,512,512]{2,1,0:T(8,128)S(1)} %copy-done, f32[1,512,512]{2,1,0:T(8,128)S(1)} %copy-done.1, f32[1,512,512]{2,1,0:T(8,128)S(1)} %copy-done.2, f32[1,512,512]{2,1,0:T(8,128)S(1)} %copy-done.3, ...), custom_call_target="tpu_custom_call" | custom-call | tf_op jit(solution)/shard_map/local_update/pallas_call | solution.py:182
  52.6 0.0 copy-start.6
  52.7 0.6 copy-done.6
  53.3 12.2 %spread_update.1 = bf16[8,64,512]{2,1,0:T(8,128)(2,1)S(1)} custom-call(s32[1,8]{1,0:T(1,128)S(1)} %copy-done.6, bf16[512,512]{1,0:T(8,128)(2,1)S(1)} %get-tuple-element.7.u_ref, f32[8,128]{1,0:T(8,128)S(1)} %get-tuple-element.8.s_ref), custom_call_target="tpu_custom_call" | custom-call | tf_op jit(solution)/shard_map/spread_update/pallas_call | solution.py:341
  65.5 0.8 %copy.9 = bf16[8,64,512]{2,1,0:T(8,128)(2,1)} copy(bf16[8,64,512]{2,1,0:T(8,128)(2,1)S(1)} %spread_update.1) | data formatting | bytes 1048576
Async XLA Ops:
  0.0 12.8 %copy-start = (f32[1,512,512]{2,1,0:T(8,128)S(1)}, f32[1,512,512]{2,1,0:T(8,128)}, u32[]{:S(2)}) copy-start(f32[1,512,512]{2,1,0:T(8,128)} %l_ref.1) | copy-start | bytes 3145732
  0.0 1.1 %copy-start.4 = (bf16[8,64,512]{2,1,0:T(8,128)(2,1)S(1)}, bf16[8,64,512]{2,1,0:T(8,128)(2,1)}, u32[]{:S(2)}) copy-start(bf16[8,64,512]{2,1,0:T(8,128)(2,1)} %g_ref.1) | copy-start | bytes 1572868
  1.1 0.7 copy-start.5
  12.8 1.2 %copy-start.1 = (f32[1,512,512]{2,1,0:T(8,128)S(1)}, f32[1,512,512]{2,1,0:T(8,128)}, u32[]{:S(2)}) copy-start(f32[1,512,512]{2,1,0:T(8,128)} %r_ref.1) | copy-start | bytes 3145732
  14.0 1.2 %copy-start.2 = (f32[1,512,512]{2,1,0:T(8,128)S(1)}, f32[1,512,512]{2,1,0:T(8,128)}, u32[]{:S(2)}) copy-start(f32[1,512,512]{2,1,0:T(8,128)} %ql_ref.1) | copy-start | bytes 3145732
  15.2 1.2 %copy-start.3 = (f32[1,512,512]{2,1,0:T(8,128)S(1)}, f32[1,512,512]{2,1,0:T(8,128)}, u32[]{:S(2)}) copy-start(f32[1,512,512]{2,1,0:T(8,128)} %qr_ref.1) | copy-start | bytes 3145732
  52.6 0.7 copy-start.6

commit v3 on v2

--- a/solution.py
+++ b/solution.py
@@ -46,11 +46,6 @@
 
 def row_copy(x, at):
     return jnp.broadcast_to(x[at : at + 1, :], x.shape)
-
-
-def reciprocal(x):
-    guess = pl.reciprocal(x, approx=True)
-    return guess * (2.0 - x * guess)
 
 
 def root_reciprocal(x):
@@ -69,19 +64,17 @@
         left, right = columns[j], columns[j + 1]
         a, b, c = row_copy(left, j), row_copy(left, j + 1), row_copy(right, j + 1)
         det = a * c - b * b
-        inv = reciprocal(det)
-        ia, ib, ic = c * inv, b * inv, a * inv
+        inv = pl.reciprocal(det, approx=True)
         root = root_reciprocal(a)
         tail = root_reciprocal(det * root * root)
         is_first, is_second = row_id == j, row_id == j + 1
+        left = left - jnp.where(is_first, 1.0, 0.0)
+        right = right - jnp.where(is_second, 1.0, 0.0)
 
         def eliminate(x):
             upper, lower = row_copy(x, j), row_copy(x, j + 1)
-            new_upper = ia * upper - ib * lower
-            new_lower = ic * lower - ib * upper
-            rest = x - left * new_upper - right * new_lower
-            new = jnp.where(is_first, new_upper, jnp.where(is_second, new_lower, rest))
-            return new, upper, lower
+            part = left * (c * upper - b * lower) + right * (a * lower - b * upper)
+            return x - part * inv, upper, lower
 
         for l in range(j + 2, tile):
             columns[l] = eliminate(columns[l])[0]
@@ -178,15 +171,17 @@
 
 def local(gradient, *states):
     width = gradient.shape[0]
-    vmem = pl.BlockSpec(memory_space=pltpu.VMEM)
+    flat = pl.BlockSpec((width, width), lambda i: (0, 0))
+    state = pl.BlockSpec((1, width, width), lambda i: (0, 0, 0))
     return pl.pallas_call(
         local_kernel,
+        grid=(1,),
         out_shape=(
             jax.ShapeDtypeStruct((width, width), jnp.bfloat16),
             jax.ShapeDtypeStruct((8, 128), jnp.float32),
         ),
-        in_specs=[vmem] * 6,
-        out_specs=(vmem, vmem),
+        in_specs=[flat] + [state] * 5,
+        out_specs=(flat, pl.BlockSpec((8, 128), lambda i: (0, 0))),
         scratch_shapes=[
             pltpu.VMEM((2, width, width), jnp.float32),
             pltpu.VMEM((2, width, width), jnp.bfloat16),

time: 67.2 us -> 65 us (0.967)
  Pallas kernels: 59.4 us -> 57.2 us
    pallas_call x1, Pallas kernels: 36.2 us -> 34 us  [local(): pl.pallas_call(local_kernel, grid=(1,), out_shape=(jax.ShapeDtypeStruct((...]
where the time goes in v3:
time: 65 us; the launch traced here: 64.2 us
  Pallas kernels  57.2 us (88%)
  local copies, waits for them, and re-layouts  6.9 us (11%)
    pallas_call x1, Pallas kernels, local(): pl.pallas_call(local_kernel, grid=(1,), out_shape=(jax.ShapeDtypeStruct((...  34 us
    pallas_call x1, Pallas kernels, spread(): pl.pallas_call(functools.partial(spread_kernel, count, groups), out_shape...  12.2 us
    pallas_call x1, Pallas kernels, collect(): pl.pallas_call(functools.partial(collect_kernel, count), out_shape=jax.Sh...  11 us
    unnamed x15, local copies, waits for them, and re-layouts  6.9 us

profile of v3, /device:TPU:0, one launch (start us, length us, event | category | flops | bytes accessed | tf_op | source)
XLA Modules:
  0.0 64.2 jit_solution(2002702927062287750)
XLA Ops:
  0.0 0.0 copy-start
  0.0 0.0 copy-start.4
  0.0 1.1 %copy-done.4 = bf16[8,64,512]{2,1,0:T(8,128)(2,1)S(1)} copy-done((bf16[8,64,512]{2,1,0:T(8,128)(2,1)S(1)}, bf16[8,64,512]{2,1,0:T(8,128)(2,1)}, u32[]{:S(2)}) %copy-start.4) | copy-done | bytes 524312
  1.1 0.0 copy-start.5
  1.1 0.7 %copy-done.5 = s32[1,8]{1,0:T(1,128)S(1)} copy-done((s32[1,8]{1,0:T(1,128)S(1)}, s32[1,8]{1,0:T(1,128)}, u32[]{:S(2)}) %copy-start.5) | copy-done | bytes 56
  1.8 11.0 %collect_gradient.1.g_ref = bf16[512,512]{1,0:T(8,128)(2,1)S(1)} custom-call(s32[1,8]{1,0:T(1,128)S(1)} %copy-done.5, bf16[8,64,512]{2,1,0:T(8,128)(2,1)S(1)} %copy-done.4), custom_call_target="tpu_custom_call" | custom-call | tf_op jit(solution)/shard_map/collect_gradient/pallas_call | solution.py:252
  12.8 0.0 copy-done
  12.8 0.0 copy-start.1
  12.8 1.2 %copy-done.1 = f32[1,512,512]{2,1,0:T(8,128)S(1)} copy-done((f32[1,512,512]{2,1,0:T(8,128)S(1)}, f32[1,512,512]{2,1,0:T(8,128)}, u32[]{:S(2)}) %copy-start.1) | copy-done | bytes 1048600
  14.0 0.0 copy-start.2
  14.0 1.2 %copy-done.2 = f32[1,512,512]{2,1,0:T(8,128)S(1)} copy-done((f32[1,512,512]{2,1,0:T(8,128)S(1)}, f32[1,512,512]{2,1,0:T(8,128)}, u32[]{:S(2)}) %copy-start.2) | copy-done | bytes 1048600
  15.2 0.0 copy-start.3
  15.2 1.2 %copy-done.3 = f32[1,512,512]{2,1,0:T(8,128)S(1)} copy-done((f32[1,512,512]{2,1,0:T(8,128)S(1)}, f32[1,512,512]{2,1,0:T(8,128)}, u32[]{:S(2)}) %copy-start.3) | copy-done | bytes 1048600
  16.5 34.0 %local_update.1 = (bf16[512,512]{1,0:T(8,128)(2,1)S(1)}, f32[8,128]{1,0:T(8,128)S(1)}) custom-call(bf16[512,512]{1,0:T(8,128)(2,1)S(1)} %collect_gradient.1.g_ref, f32[1,512,512]{2,1,0:T(8,128)S(1)} %copy-done, f32[1,512,512]{2,1,0:T(8,128)S(1)} %copy-done.1, f32[1,512,512]{2,1,0:T(8,128)S(1)} %copy-done.2, f32[1,512,512]{2,1,0:T(8,128)S(1)} %copy-done.3, ...), custom_call_target="tpu_custom_call" | custom-call | tf_op jit(solution)/shard_map/local_update/pallas_call | solution.py:176
  50.5 0.0 copy-start.6
  50.5 0.6 %copy-done.6 = s32[1,8]{1,0:T(1,128)S(1)} copy-done((s32[1,8]{1,0:T(1,128)S(1)}, s32[1,8]{1,0:T(1,128)}, u32[]{:S(2)}) %copy-start.6) | copy-done | bytes 56
  51.1 12.2 %spread_update.1 = bf16[8,64,512]{2,1,0:T(8,128)(2,1)S(1)} custom-call(s32[1,8]{1,0:T(1,128)S(1)} %copy-done.6, bf16[512,512]{1,0:T(8,128)(2,1)S(1)} %get-tuple-element.7.u_ref, f32[8,128]{1,0:T(8,128)S(1)} %get-tuple-element.8.s_ref), custom_call_target="tpu_custom_call" | custom-call | tf_op jit(solution)/shard_map/spread_update/pallas_call | solution.py:336
  63.4 0.8 %copy.9 = bf16[8,64,512]{2,1,0:T(8,128)(2,1)} copy(bf16[8,64,512]{2,1,0:T(8,128)(2,1)S(1)} %spread_update.1) | data formatting | bytes 1048576
Async XLA Ops:
  0.0 12.8 %copy-start = (f32[1,512,512]{2,1,0:T(8,128)S(1)}, f32[1,512,512]{2,1,0:T(8,128)}, u32[]{:S(2)}) copy-start(f32[1,512,512]{2,1,0:T(8,128)} %l_ref.1) | copy-start | bytes 3145732
  0.0 1.1 %copy-start.4 = (bf16[8,64,512]{2,1,0:T(8,128)(2,1)S(1)}, bf16[8,64,512]{2,1,0:T(8,128)(2,1)}, u32[]{:S(2)}) copy-start(bf16[8,64,512]{2,1,0:T(8,128)(2,1)} %g_ref.1) | copy-start | bytes 1572868
  1.1 0.7 %copy-start.5 = (s32[1,8]{1,0:T(1,128)S(1)}, s32[1,8]{1,0:T(1,128)}, u32[]{:S(2)}) copy-start(s32[1,8]{1,0:T(1,128)} %owners_ref.3) | copy-start | bytes 100
  12.8 1.2 %copy-start.1 = (f32[1,512,512]{2,1,0:T(8,128)S(1)}, f32[1,512,512]{2,1,0:T(8,128)}, u32[]{:S(2)}) copy-start(f32[1,512,512]{2,1,0:T(8,128)} %r_ref.1) | copy-start | bytes 3145732
  14.0 1.2 %copy-start.2 = (f32[1,512,512]{2,1,0:T(8,128)S(1)}, f32[1,512,512]{2,1,0:T(8,128)}, u32[]{:S(2)}) copy-start(f32[1,512,512]{2,1,0:T(8,128)} %ql_ref.1) | copy-start | bytes 3145732
  15.2 1.2 %copy-start.3 = (f32[1,512,512]{2,1,0:T(8,128)S(1)}, f32[1,512,512]{2,1,0:T(8,128)}, u32[]{:S(2)}) copy-start(f32[1,512,512]{2,1,0:T(8,128)} %qr_ref.1) | copy-start | bytes 3145732
  50.5 0.7 %copy-start.6 = (s32[1,8]{1,0:T(1,128)S(1)}, s32[1,8]{1,0:T(1,128)}, u32[]{:S(2)}) copy-start(s32[1,8]{1,0:T(1,128)} %owners_ref.3) | copy-start | bytes 100
